TPU v7x, 32 devices: a whole 2x2x4 slice. The times are simulated.
32 devices in a mesh: cfg: 2 (over x), space: 8 (over z, y), diag: 2 (over core).
Axes of the slice: x: 2, y: 2, z: 4, core: 2. Of those that a mesh axis runs over, the one named last changes fastest.
Arguments:
- eigvecs: bfloat16 [8, 2, 3, 128, 16, 256], P('cfg', None, None, None, ('space', 'diag')), parts along dimension 0, may hold values from -6 to 6
- gauge_links: float32 [8, 3, 2, 3, 3, 16, 256], P('cfg', None, None, None, None, ('space', 'diag')), parts along dimension 0, may hold values from -6 to 6
- momenta: int32 [4, 3], replicated, may hold values from -2 to 2
- spin_mix: float32 [16, 4, 4], replicated, may hold values from -4 to 4
- perambulators: bfloat16 [64, 4, 2, 128, 512], P(('cfg', 'space', 'diag')), parts along dimension 0, may hold values from -0.375 to 0.375
- contraction_list: int32 [32, 3], P(('space', 'diag')), may hold values from 0 to 63, as said below
Outputs:
- diagrams: bfloat16 [64, 4, 2, 128, 512], P(('cfg', 'space', 'diag')), parts along dimension 0
There are 2 independent parts, one for each index of `cfg`. A program takes and returns all parts, laid end to end along the dimension named above; an argument that names none is the same for every part. Nothing has to cross between parts.
Inputs may be any that keep to these rules, and one draw needn't show every extreme that they name: `contraction_list`: row j is one diagram. Column 0 is an elemental item below 64, column 1 a spin structure below 16, column 2 a perambulator q with q // 2 == j // 2; each aligned group of 2 rows names each of its 2 perambulators exactly once.
All inputs are finite; a program needn't handle non-finite values.
Results may differ from a plain program's by a relative error of at most 0.0064.
Values may be sent and summed in bfloat16 or wider, within the bound.
No kernel may reach another device: no remote copies, remote signals or barrier semaphores. Data moves between devices by JAX's collectives and lax.ppermute only.
A program may use at most 128 MiB of HBM per device.

v0:
```python
import functools
import math

import jax
import jax.numpy as jnp
from jax import lax
from jax.experimental import pallas as pl
from jax.experimental.pallas import tpu as pltpu
from jax.sharding import PartitionSpec as P

NCOL = 3
NMOM = 4
NDISP = 4
LX = 16
LY = 16
LANES = 128
ROWS = 16
SITES = ("space", "diag")
MIB = 1024 * 1024
PLANE_LIMIT = 24 * MIB


def shifted(value, axis, by):
    size = lax.axis_size(axis)
    return lax.ppermute(value, axis, [(i, (i + by) % size) for i in range(size)])


def in_hbm(value):
    return pltpu.with_memory_space_constraint(value, pltpu.HBM)


def exchanged(value, mask):
    size = lax.axis_size(SITES)
    return lax.ppermute(value, SITES, [(i, i ^ mask) for i in range(size)])


def gathered(rows, early, late):
    bits = lax.axis_size(SITES).bit_length() - 1
    value = rows[None]
    for low in range(0, bits, 2):
        if low == 2:
            value, late = lax.optimization_barrier((value, late))
        arrived = [exchanged(value, step << low) for step in range(1, 1 << min(2, bits - low))]
        if low == 0:
            arrived, early = lax.optimization_barrier((arrived, early))
        value = jnp.concatenate([value] + arrived)
    return value, early, late


def color_product(matrix, real, imag, adjoint):
    rows = []
    for row in range(NCOL):
        real_part = imag_part = None
        for col in range(NCOL):
            if adjoint:
                mreal, mimag = matrix[0][col][row], matrix[1][col][row]
                one = mreal * real[col] + mimag * imag[col]
                two = mreal * imag[col] - mimag * real[col]
            else:
                mreal, mimag = matrix[0][row][col], matrix[1][row][col]
                one = mreal * real[col] - mimag * imag[col]
                two = mreal * imag[col] + mimag * real[col]
            real_part = one if real_part is None else real_part + one
            imag_part = two if imag_part is None else imag_part + two
        rows.append((real_part, imag_part))
    return rows


def color_loop(link, nvec, width, load, store, adjoint):
    height = math.gcd(nvec, 2 * ROWS)
    for lane in range(0, width, LANES):
        lanes = pl.ds(lane, LANES)
        matrix = [
            [[link(part, row, col, lanes) for col in range(NCOL)] for row in range(NCOL)] for part in range(2)
        ]
        for start in range(0, nvec, height):
            rows = pl.ds(start, height)
            real = [load(0, color, rows, lanes) for color in range(NCOL)]
            imag = [load(1, color, rows, lanes) for color in range(NCOL)]
            for color, (one, two) in enumerate(color_product(matrix, real, imag, adjoint)):
                store(0, color, rows, lanes, one)
                store(1, color, rows, lanes, two)


def fill_tables(position, total_z, plane, momenta_ref, phase_ref, turn_ref):
    width = phase_ref.shape[-1]
    flat = lax.broadcasted_iota(jnp.int32, (1, width), 1)
    xcoord = (flat % LX).astype(jnp.float32)
    ycoord = (flat % plane // LX).astype(jnp.float32)
    zcoord = (position * (width // plane) + flat // plane).astype(jnp.float32)
    for moment in range(NMOM):
        along_x = momenta_ref[moment, 0].astype(jnp.float32)
        along_y = momenta_ref[moment, 1].astype(jnp.float32)
        along_z = momenta_ref[moment, 2].astype(jnp.float32)
        angle = (
            2.0 * math.pi * (along_x * xcoord / LX + along_y * ycoord / LY + along_z * zcoord / total_z)
        )
        phase_ref[moment, 0] = jnp.cos(angle)
        phase_ref[moment, 1] = jnp.sin(angle)
        turn = jnp.full((1, turn_ref.shape[-1]), 2.0 * math.pi / total_z, jnp.float32) * along_z
        turn_ref[moment, 0] = jnp.cos(turn)
        turn_ref[moment, 1] = jnp.sin(turn)


def fill_moves(move_ref):
    width = move_ref.shape[-1]
    source = lax.broadcasted_iota(jnp.int32, (width, width), 0)
    site = lax.broadcasted_iota(jnp.int32, (width, width), 1)
    xcoord = site % LX
    ycoord = site // LX % LY
    for sign, by in enumerate((1, -1)):
        along_x = site - xcoord + (xcoord + LX + by) % LX
        along_y = site + ((ycoord + LY + by) % LY - ycoord) * LX
        move_ref[0, sign] = (source == along_x).astype(jnp.float32).astype(jnp.bfloat16)
        move_ref[1, sign] = (source == along_y).astype(jnp.float32).astype(jnp.bfloat16)


def plane_kernel(
    total_z, plane, scale,
    position_ref, momenta_in, vector_in, link_in,
    item_ref, own_ref, phase_ref, turn_ref,
    momenta_ref, vector_ref, link_ref,
    ahead_x_ref, ahead_y_ref, behind_x_ref, behind_y_ref, adjoint_x_ref, adjoint_y_ref,
    phased_ref, still_ref, moved_x_ref, moved_y_ref, move_ref, momenta_sem, sems,
):
    now = pl.program_id(0)
    slices, _, _, nvec, width = vector_ref.shape

    def copies(index):
        return (
            pltpu.make_async_copy(vector_in.at[index], vector_ref.at[index], sems.at[0, index]),
            pltpu.make_async_copy(link_in.at[index], link_ref.at[index], sems.at[1, index]),
        )

    @pl.when(now == 0)
    def _():
        moments = pltpu.make_async_copy(momenta_in, momenta_ref, momenta_sem)
        moments.start()
        for index in range(slices):
            for copy in copies(index):
                copy.start()
        fill_moves(move_ref)
        moments.wait()
        fill_tables(position_ref[0], total_z, plane, momenta_ref, phase_ref, turn_ref)

    for copy in copies(now):
        copy.wait()

    def linker(direction):
        return lambda part, row, col, lanes: link_ref[now, direction, part, row, col, :, lanes]

    def vector(part, color, rows, lanes):
        return vector_ref[now, part, color, rows, lanes].astype(jnp.float32)

    def gram(moved_ref, disp):
        product = lax.dot_general(
            phased_ref[...], moved_ref[...], (((1,), (1,)), ((), ())), preferred_element_type=jnp.float32
        )
        for moment in range(NMOM):
            start = 2 * moment * nvec
            upper = product[start : start + nvec]
            lower = product[start + nvec : start + 2 * nvec]
            factor = scale if disp == 0 else 0.5 * scale
            item_ref[0, moment, disp, 0] = (factor * (upper[:, :nvec] + lower[:, nvec:])).astype(item_ref.dtype)
            item_ref[0, moment, disp, 1] = (factor * (upper[:, nvec:] - lower[:, :nvec])).astype(item_ref.dtype)

    flat = vector_ref[now].reshape(2 * NCOL * nvec, width)
    for direction, ahead_ref in enumerate((ahead_x_ref, ahead_y_ref)):
        ahead_ref[...] = jnp.dot(
            flat, move_ref[direction, 0], preferred_element_type=jnp.float32
        ).reshape(ahead_ref.shape)

    for color in range(NCOL):
        span = pl.ds(color * width, width)
        for part in range(2):
            still_ref[pl.ds(part * nvec, nvec), span] = vector_ref[now, part, color]
        for start in range(0, nvec, ROWS):
            real = vector_ref[now, 0, color, pl.ds(start, ROWS), :].astype(jnp.float32)
            imag = vector_ref[now, 1, color, pl.ds(start, ROWS), :].astype(jnp.float32)
            for moment in range(NMOM):
                cosine = phase_ref[moment, 0]
                sine = phase_ref[moment, 1]
                first = 2 * moment * nvec + start
                phased_ref[pl.ds(first, ROWS), span] = (cosine * real - sine * imag).astype(jnp.bfloat16)
                phased_ref[pl.ds(first + nvec, ROWS), span] = (sine * real + cosine * imag).astype(jnp.bfloat16)
    gram(still_ref, 0)

    for direction, (adjoint_ref, behind_ref) in enumerate(
        ((adjoint_x_ref, behind_x_ref), (adjoint_y_ref, behind_y_ref))
    ):

        def adjoint(part, color, rows, lanes, value):
            adjoint_ref[part, color, rows, lanes] = value.astype(jnp.bfloat16)

        color_loop(linker(direction), nvec, width, vector, adjoint, True)
        behind_ref[...] = jnp.dot(
            adjoint_ref[...].reshape(2 * NCOL * nvec, width),
            move_ref[direction, 1],
            preferred_element_type=jnp.float32,
        ).reshape(behind_ref.shape)

    for direction, (ahead_ref, behind_ref, moved_ref) in enumerate(
        ((ahead_x_ref, behind_x_ref, moved_x_ref), (ahead_y_ref, behind_y_ref, moved_y_ref))
    ):

        def ahead(part, color, rows, lanes):
            return ahead_ref[part, color, rows, lanes]

        def forward(part, color, rows, lanes, value):
            moved_ref[
                pl.ds(part * nvec + rows.start, rows.size), pl.ds(color * width + lanes.start, lanes.size)
            ] = (value - behind_ref[part, color, rows, lanes]).astype(jnp.bfloat16)

        color_loop(linker(direction), nvec, width, ahead, forward, False)
        gram(moved_ref, direction + 1)

    def own(part, color, rows, lanes, value):
        own_ref[0, part, color, rows, lanes] = value

    color_loop(linker(2), nvec, width, vector, own, True)


def plane_items(position, momenta, vectors, links, total_z, plane, scale):
    slices, _, _, nvec, width = vectors.shape
    color_block = (2, NCOL, nvec, width)
    return pl.pallas_call(
        functools.partial(plane_kernel, total_z, plane, scale),
        grid=(slices,),
        in_specs=[pl.BlockSpec(memory_space=pltpu.SMEM)] + [pl.BlockSpec(memory_space=pltpu.HBM)] * 3,
        out_specs=[
            pl.BlockSpec((1, NMOM, NDISP - 1, 2, nvec, nvec), lambda t: (t, 0, 0, 0, 0, 0)),
            pl.BlockSpec((1,) + color_block, lambda t: (t, 0, 0, 0, 0)),
            pl.BlockSpec((NMOM, 2, 1, width), lambda t: (0, 0, 0, 0)),
            pl.BlockSpec((NMOM, 2, 1, nvec), lambda t: (0, 0, 0, 0)),
        ],
        out_shape=[
            jax.ShapeDtypeStruct((slices, NMOM, NDISP - 1, 2, nvec, nvec), jnp.bfloat16),
            jax.ShapeDtypeStruct(vectors.shape, jnp.float32),
            jax.ShapeDtypeStruct((NMOM, 2, 1, width), jnp.float32),
            jax.ShapeDtypeStruct((NMOM, 2, 1, nvec), jnp.float32),
        ],
        scratch_shapes=[
            pltpu.SMEM(momenta.shape, jnp.int32),
            pltpu.VMEM(vectors.shape, jnp.bfloat16),
            pltpu.VMEM(links.shape, jnp.float32),
        ]
        + [pltpu.VMEM(color_block, jnp.float32)] * 4
        + [pltpu.VMEM(color_block, jnp.bfloat16)] * 2
        + [pltpu.VMEM((NMOM * 2 * nvec, NCOL * width), jnp.bfloat16)]
        + [pltpu.VMEM((2 * nvec, NCOL * width), jnp.bfloat16)] * 3
        + [
            pltpu.VMEM((2, 2, width, width), jnp.bfloat16),
            pltpu.SemaphoreType.DMA,
            pltpu.SemaphoreType.DMA((2, slices)),
        ],
        compiler_params=pltpu.CompilerParams(vmem_limit_bytes=PLANE_LIMIT),
        cost_estimate=pl.CostEstimate(
            flops=slices * 16 * NMOM * nvec * nvec * NCOL * width,
            bytes_accessed=6 * vectors.size + 4 * links.size,
            transcendentals=0,
        ),
        name="plane_items",
    )(position, in_hbm(momenta), in_hbm(vectors), in_hbm(links))


def layer_kernel(
    core, scale, rows_ref, item_ref, own_ref, ahead_ref, phase_ref, turn_ref, out_ref, lhs_ref, listed_ref
):
    nvec, width = own_ref.shape[3:]
    total = out_ref.shape[0]
    sites = rows_ref.shape[0] // 2

    def parts_of(place):
        item = rows_ref[2 * lax.rem(place, sites) + core, lax.div(place, sites), 0]
        rest = lax.rem(item, NMOM * NDISP)
        return lax.div(item, NMOM * NDISP), lax.div(rest, NDISP), lax.rem(rest, NDISP)

    def bond(place, lhs):
        slice_index, moment, _ = parts_of(place)
        cosine = phase_ref[moment, 0]
        sine = phase_ref[moment, 1]
        for color in range(NCOL):
            span = pl.ds(color * width, width)
            for part in range(2):
                value = own_ref[slice_index, part, color]
                lhs[pl.ds(part * nvec, nvec), span] = (cosine * value).astype(jnp.bfloat16)
                lhs[pl.ds((2 + part) * nvec, nvec), span] = (sine * value).astype(jnp.bfloat16)
        rhs = jnp.concatenate(
            [
                jnp.concatenate([ahead_ref[slice_index, part, color] for color in range(NCOL)], 1)
                for part in range(2)
            ],
            0,
        )
        gram = lax.dot_general(lhs[...], rhs, (((1,), (1,)), ((), ())), preferred_element_type=jnp.float32)
        block = [
            [gram[i * nvec : (i + 1) * nvec, j * nvec : (j + 1) * nvec] for j in range(2)] for i in range(4)
        ]
        cos_real = block[0][0] + block[1][1]
        cos_imag = block[0][1] - block[1][0]
        sin_real = block[2][0] + block[3][1]
        sin_imag = block[2][1] - block[3][0]
        half = 0.5 * scale
        turn_cos = half * turn_ref[moment, 0]
        turn_sin = half * turn_ref[moment, 1]
        back_real = cos_real - sin_imag
        back_imag = cos_imag + sin_real
        real = half * (cos_real + sin_imag) - (turn_cos * back_real - turn_sin * back_imag).T
        imag = half * (cos_imag - sin_real) + (turn_cos * back_imag + turn_sin * back_real).T
        return real.astype(out_ref.dtype), imag.astype(out_ref.dtype)

    found = jnp.int32(0)
    for place in range(total):
        slice_index, moment, disp = parts_of(jnp.int32(place))
        out_ref[place] = item_ref[slice_index, moment, jnp.minimum(disp, NDISP - 2)]
        listed_ref[found] = place
        found = found + (disp == NDISP - 1).astype(jnp.int32)

    @pl.loop(0, lax.div(found + 1, 2))
    def _(pair):
        both = [listed_ref[2 * pair], listed_ref[jnp.minimum(2 * pair + 1, found - 1)]]
        results = [bond(place, lhs_ref.at[index]) for index, place in enumerate(both)]
        for place, (real, imag) in zip(both, results):
            out_ref[place, 0] = real
            out_ref[place, 1] = imag


def layer_items(core, rows, item, own, ahead, phase, turn, scale):
    slices, _, _, nvec, width = own.shape
    devices, slots, _ = rows.shape
    total = slots * devices // 2
    whole = pl.BlockSpec(memory_space=pltpu.VMEM)
    return pl.pallas_call(
        functools.partial(layer_kernel, core, scale),
        in_specs=[pl.BlockSpec(memory_space=pltpu.SMEM)] + [whole] * 5,
        out_specs=whole,
        out_shape=jax.ShapeDtypeStruct((total, 2, nvec, nvec), jnp.bfloat16),
        scratch_shapes=[
            pltpu.VMEM((2, 4 * nvec, NCOL * width), jnp.bfloat16),
            pltpu.SMEM((total,), jnp.int32),
        ],
        compiler_params=pltpu.CompilerParams(vmem_limit_bytes=12 * MIB),
        cost_estimate=pl.CostEstimate(
            flops=total * 4 * nvec * nvec * NCOL * width,
            bytes_accessed=2 * own.size,
            transcendentals=0,
        ),
        name="layer_items",
    )(rows, item, own, ahead, phase, turn)


def add_kernel(places, *refs):
    terms, outs = refs[: len(places[0][0])], refs[len(places[0][0]) :]
    for out_ref, wanted in zip(outs, places):
        for entry, at in enumerate(wanted):
            total = terms[0][at[0]].astype(jnp.float32)
            for ref, index in zip(terms[1:], at[1:]):
                total = total + ref[index].astype(jnp.float32)
            out_ref[entry] = total.astype(out_ref.dtype)


def added(terms, sent, kept=()):
    groups = [(sent, jnp.bfloat16)] + [(kept, jnp.float32)] * bool(kept)
    places = [[tuple(entries.index(r) for entries, _ in terms) for r in group] for group, _ in groups]
    values = [value for _, value in terms]
    tail = values[0].shape[1:]
    whole = pl.BlockSpec(memory_space=pltpu.VMEM)
    size = (len(sent) + len(kept)) * math.prod(tail)
    return pl.pallas_call(
        functools.partial(add_kernel, places),
        in_specs=[whole] * len(values),
        out_specs=[whole] * len(groups),
        out_shape=[jax.ShapeDtypeStruct((len(group),) + tail, dtype) for group, dtype in groups],
        compiler_params=pltpu.CompilerParams(vmem_limit_bytes=8 * MIB),
        cost_estimate=pl.CostEstimate(
            flops=len(values) * size, bytes_accessed=2 * (len(values) + 1) * size, transcendentals=0
        ),
        name="added",
    )(*values)


def halved(terms, wanted, bit):
    far = [(slot, r ^ (1 << (bit - 1))) for slot, r in wanted]
    leaving, left = added(terms, far, wanted)
    return [(wanted, left), (wanted, exchanged(leaving, 1 << bit))]


def chunked(terms, slot, order):
    entries = [entry for entry in terms[0][0] if entry[0] == slot]
    for place, bit in enumerate(order[:-2]):
        entries = [(slot, r) for _, r in entries if not r >> (bit - 1) & 1]
        if place < len(order) - 3:
            terms = halved(terms, entries, bit)
    middle = len(entries) // 2
    return [functools.partial(halved, terms, chunk, order[-3]) for chunk in (entries[middle:], entries[:middle])]


def sent(terms):
    entries = terms[0][0]
    arrived = []
    for slot, r in reversed(entries):
        if r == 0:
            break
        own = [(slot, 0)] if entries[0][1] == 0 and (slot, r) == entries[1] else []
        outs = added(terms, [(slot, r)], own)
        arrived.append(exchanged(outs[0], 2 * r))
    return arrived + list(outs[1:])


def mix_kernel(slot_ref, structure_ref, weight_ref, tau_ref, out_ref):
    spins, _, nvec, width = tau_ref.shape[1:]
    base = structure_ref[pl.program_id(0)] * spins * spins
    weight = [[weight_ref[base + r * spins + s] for s in range(spins)] for r in range(spins)]

    @pl.loop(0, 2 * nvec // ROWS)
    def _(index):
        part = index // (nvec // ROWS)
        rows = pl.ds(pl.multiple_of(index % (nvec // ROWS) * ROWS, ROWS), ROWS)
        tau = [tau_ref[0, s, part, rows, :].astype(jnp.float32) for s in range(spins)]
        for r in range(spins):
            mixed = weight[r][0] * tau[0]
            for s in range(1, spins):
                mixed = mixed + weight[r][s] * tau[s]
            out_ref[0, r, part, rows, :] = mixed.astype(jnp.bfloat16)


def mixed_perambulators(slots, structures, weights, perambulators):
    block = (1,) + perambulators.shape[1:]
    count = slots.shape[0]
    return pl.pallas_call(
        mix_kernel,
        grid_spec=pltpu.PrefetchScalarGridSpec(
            num_scalar_prefetch=3,
            grid=(count,),
            in_specs=[pl.BlockSpec(block, lambda j, slot, *_: (slot[j], 0, 0, 0, 0))],
            out_specs=pl.BlockSpec(block, lambda j, *_: (j, 0, 0, 0, 0)),
        ),
        out_shape=jax.ShapeDtypeStruct((count,) + perambulators.shape[1:], jnp.bfloat16),
        compiler_params=pltpu.CompilerParams(vmem_limit_bytes=8 * MIB),
        cost_estimate=pl.CostEstimate(
            flops=8 * perambulators.size, bytes_accessed=4 * perambulators.size, transcendentals=0
        ),
        name="mixed_perambulators",
    )(slots, structures, weights, in_hbm(perambulators))


def diagram_kernel(owners, *refs):
    terms = refs[:-4]
    tau_ref, out_ref, block_ref, sems = refs[-4:]
    spins, _, nvec, width = tau_ref.shape[1:]
    count = tau_ref.shape[0]

    def copy(index, r):
        return pltpu.make_async_copy(block_ref.at[index, r], out_ref.at[index, r], sems.at[index, r])

    for index in range(count):
        real, imag = (
            sum(ref[0, part].astype(jnp.float32) for ref, owner in zip(terms, owners) if owner == index)
            for part in range(2)
        )
        square = jnp.concatenate(
            [jnp.concatenate([real, -imag], 1), jnp.concatenate([imag, real], 1)], 0
        ).astype(jnp.bfloat16)
        for r in range(spins):
            tau = tau_ref[index, r].reshape(2 * nvec, width)
            block = jnp.dot(square, tau, preferred_element_type=jnp.float32)
            block_ref[index, r] = block.astype(jnp.bfloat16).reshape(2, nvec, width)
            copy(index, r).start()
    for index in range(count):
        for r in range(spins):
            copy(index, r).wait()


def diagrams(owners, terms, tau):
    count, spins, _, nvec, width = tau.shape
    whole = pl.BlockSpec(memory_space=pltpu.VMEM)
    return pl.pallas_call(
        functools.partial(diagram_kernel, owners),
        in_specs=[whole] * (len(terms) + 1),
        out_specs=pl.BlockSpec(memory_space=pltpu.HBM),
        out_shape=jax.ShapeDtypeStruct(tau.shape, jnp.bfloat16),
        scratch_shapes=[
            pltpu.VMEM(tau.shape, jnp.bfloat16),
            pltpu.SemaphoreType.DMA((count, spins)),
        ],
        compiler_params=pltpu.CompilerParams(vmem_limit_bytes=12 * MIB),
        cost_estimate=pl.CostEstimate(
            flops=8 * nvec * nvec * width * spins * count, bytes_accessed=4 * tau.size, transcendentals=0
        ),
        name="diagrams",
    )(*terms, tau)


def body(eigvecs, gauge_links, momenta, spin_mix, perambulators, contraction_list):
    slices, _, _, nvec, depth, plane = eigvecs.shape
    devices = lax.axis_size(SITES)
    position = lax.axis_index(SITES)
    bits = devices.bit_length() - 1
    total_z = depth * devices
    width = depth * plane
    scale = 1.0 / math.sqrt(NCOL * plane * total_z)
    place = position.reshape(1)
    rows, after, place = gathered(contraction_list, eigvecs, place)
    upper = shifted(after[:, :, :, :, :1, :], SITES, -1)
    vectors = eigvecs.reshape(slices, 2, NCOL, nvec, width)
    links = gauge_links.reshape(slices, 3, 2, NCOL, NCOL, 1, width)
    item, own, phase, turn = plane_items(place, momenta, vectors, links, total_z, plane, scale)
    chosen = contraction_list[:, 2] - position * perambulators.shape[0]
    tau = mixed_perambulators(chosen, contraction_list[:, 1], spin_mix.reshape(-1), perambulators)
    ahead = jnp.concatenate([eigvecs[:, :, :, :, 1:, :], upper], 4).reshape(vectors.shape)
    send = layer_items(1, rows, item, own, ahead, phase, turn, scale)
    keep = layer_items(0, rows, item, own, ahead, phase, turn, scale)
    slots = range(contraction_list.shape[0])
    entries = [(slot, r) for slot in slots for r in range(devices // 2)]
    terms = [(entries, keep), (entries, exchanged(send, 1))]
    chunks = [
        chunked(terms, slot, [1 + (slot + step) % (bits - 1) for step in range(bits - 1)]) for slot in slots
    ]
    chunks = list(zip(*[[chunks[slot][half]() for slot in slots] for half in range(2)]))
    chunks = [list(pair) for pair in chunks]
    first = chunks[0][0]
    values, tau = lax.optimization_barrier(([value for _, value in first], tau))
    chunks[0][0] = [(left, value) for (left, _), value in zip(first, values)]
    owners = []
    parts = []
    for half in range(2):
        for slot in slots:
            values = sent(chunks[slot][half])
            owners += [slot] * len(values)
            parts += values
    return diagrams(owners, parts, tau)


def solution(mesh):
    placed = (
        P("cfg", None, None, None, ("space", "diag"), None),
        P("cfg", None, None, None, None, ("space", "diag"), None),
        P(),
        P(),
        P(("cfg", "space", "diag"), None, None, None, None),
        P(("space", "diag"), None),
    )
    return jax.shard_map(
        body,
        mesh=mesh,
        in_specs=placed,
        out_specs=P(("cfg", "space", "diag"), None, None, None, None),
        check_vma=False,
    )
```

profile of v0, /device:TPU:0, one launch (start us, length us, event | category | flops | bytes accessed | tf_op | source)
XLA Modules:
  0.0 63.0 jit_solution(9624353512806268902)
XLA Ops:
  0.5 2.5 %collective-permute-start.1 = (s32[1,2,3]{2,1,0:T(2,128)}, s32[1,2,3]{2,1,0:T(2,128)S(1)}, u32[]{:S(2)}, u32[]{:S(2)}) collective-permute-start(s32[1,2,3]{2,1,0:T(2,128)} %bitcast.8), channel_id=1, source_target_pairs={{0,2},{1,3},{2,0},{3,1},{4,6},{5,7},{6,4},{7,5},{8,10},{9,11},{10,... | collective-permute-start | bytes 80 | tf_op jit(solution)/shard_map/ppermute | solution.py:34
  3.1 1.6 %collective-permute-done.1 = s32[1,2,3]{2,1,0:T(2,128)S(1)} collective-permute-done((s32[1,2,3]{2,1,0:T(2,128)}, s32[1,2,3]{2,1,0:T(2,128)S(1)}, u32[]{:S(2)}, u32[]{:S(2)}) %collective-permute-start.1) | collective-permute-done | bytes 56 | tf_op jit(solution)/shard_map/ppermute | solution.py:34
  4.7 1.4 %collective-permute-done.2 = s32[1,2,3]{2,1,0:T(2,128)S(1)} collective-permute-done((s32[1,2,3]{2,1,0:T(2,128)}, s32[1,2,3]{2,1,0:T(2,128)S(1)}, u32[]{:S(2)}, u32[]{:S(2)}) %collective-permute-start.2) | collective-permute-done | bytes 56 | tf_op jit(solution)/shard_map/ppermute | solution.py:34
  6.2 3.4 %collective-permute-start.6 = (bf16[4,2,3,128,1,256]{5,3,2,1,0,4:T(8,128)(2,1)}, bf16[4,2,3,128,1,256]{5,3,2,1,0,4:T(8,128)(2,1)S(1)}, u32[]{:S(2)}, u32[]{:S(2)}) collective-permute-start(bf16[4,2,3,128,1,256]{5,3,2,1,0,4:T(8,128)(2,1)} %bitcast.11), channel_id=1, source_target_pairs={{0,15},{1,0},{2,1},{3,2},{4,3},{5,4},{6,5},{7,6},{8,7},{9,8},{10,9... | collective-permute-start | bytes 4718600 | tf_op jit(solution)/shard_map/ppermute | solution.py:25
  9.6 0.7 %pad_add_fusion = s32[4,2,3]{2,1,0:T(2,128)S(1)} fusion(s32[1,2,3]{2,1,0:T(2,128)S(1)} %collective-permute-done.2, s32[1,2,3]{2,1,0:T(2,128)S(1)} %collective-permute-done.1, s32[1,2,3]{2,1,0:T(2,128)S(1)} %collective-permute-done, s32[1,2,3]{2,1,0:T(2,128)} %bitcast.10), kind=kLoop, calls=%fused_computation.4 | loop fusion | flops 72 | bytes 192 | tf_op jit(solution)/shard_map/concatenate | solution.py:46
  10.2 1.0 %collective-permute-start.4 = (s32[4,2,3]{2,1,0:T(2,128)S(1)}, s32[4,2,3]{2,1,0:T(2,128)S(1)}, u32[]{:S(2)}, u32[]{:S(2)}) collective-permute-start(s32[4,2,3]{2,1,0:T(2,128)S(1)} %pad_add_fusion), channel_id=1, source_target_pairs={{0,8},{1,9},{2,10},{3,11},{4,12},{5,13},{6,14},{7,15},{8,0},{9,1},... | collective-permute-start | bytes 296 | tf_op jit(solution)/shard_map/ppermute | solution.py:34
  11.3 3.4 %collective-permute-start.5 = (s32[4,2,3]{2,1,0:T(2,128)S(1)}, s32[4,2,3]{2,1,0:T(2,128)S(1)}, u32[]{:S(2)}, u32[]{:S(2)}) collective-permute-start(s32[4,2,3]{2,1,0:T(2,128)S(1)} %pad_add_fusion), channel_id=1, source_target_pairs={{0,12},{1,13},{2,14},{3,15},{4,8},{5,9},{6,10},{7,11},{8,4},{9,5},... | collective-permute-start | bytes 296 | tf_op jit(solution)/shard_map/ppermute | solution.py:34
  14.6 14.9 %plane_items.1 = (bf16[4,4,3,2,128,128]{5,4,3,2,1,0:T(8,128)(2,1)S(1)}, f32[4,2,3,128,256]{4,3,2,1,0:T(8,128)S(1)}, f32[4,2,1,256]{3,2,1,0:T(1,128)S(1)}, f32[4,2,1,128]{3,2,1,0:T(1,128)S(1)}) custom-call(s32[1]{0:T(128)} %bitcast.1.position_ref, s32[4,3]{1,0:T(4,128)} %momenta_in.1, bf16[4,2,3,128,256]{4,3,2,1,0:T(8,128)(2,1)} %bitcast.12, ...), custom_call_target="tpu_custom_call" | custom-call | flops 3221225472 | bytes 4939776 | tf_op jit(solution)/shard_map/plane_items/pallas_call | solution.py:226
  29.6 2.5 %layer_items.3 = bf16[16,2,128,128]{3,2,1,0:T(8,128)(2,1)S(1)} custom-call(s32[16,2,3]{2,1,0:T(2,128)S(1)} %constant_dynamic-update-slice_fusion.rows_ref, bf16[4,4,3,2,128,128]{5,4,3,2,1,0:T(8,128)(2,1)S(1)} %get-tuple-element.35.item_ref, f32[4,2,3,128,256]{4,3,2,1,0:T(8,128)S(1)} %get-tuple-element.36.own_ref, bf16[4,2,3,128,256]{4,3,2,1,0:T(8,128)(2,1)S(1)} %bitcast.5, ...), custom_call_target="tpu_custom_call" | custom-call | flops 805306368 | bytes 1572864 | tf_op jit(solution)/shard_map/layer_items/pallas_call | solution.py:333
  32.1 1.1 %copy-done = bf16[4,2,3,128,1,256]{5,3,2,1,0,4:T(8,128)(2,1)} copy-done((bf16[4,2,3,128,1,256]{5,3,2,1,0,4:T(8,128)(2,1)}, bf16[4,2,3,128,1,256]{5,3,2,1,0,4:T(8,128)(2,1)S(1)}, u32[]{:S(2)}) %copy-start) | copy-done | bytes 1572888
  33.2 1.4 %copy-done.1 = bf16[4,2,3,128,1,256]{5,3,2,1,0,4:T(8,128)(2,1)S(1)} copy-done((bf16[4,2,3,128,1,256]{5,3,2,1,0,4:T(8,128)(2,1)S(1)}, bf16[4,2,3,128,1,256]{5,3,2,1,0,4:T(8,128)(2,1)}, u32[]{:S(2)}) %copy-start.1) | copy-done | bytes 1572888
  34.6 4.0 %layer_items.2.refs_0_ = bf16[16,2,128,128]{3,2,1,0:T(8,128)(2,1)S(1)} custom-call(s32[16,2,3]{2,1,0:T(2,128)S(1)} %constant_dynamic-update-slice_fusion.rows_ref, bf16[4,4,3,2,128,128]{5,4,3,2,1,0:T(8,128)(2,1)S(1)} %get-tuple-element.35.item_ref, f32[4,2,3,128,256]{4,3,2,1,0:T(8,128)S(1)} %get-tuple-element.36.own_ref, ...), custom_call_target="tpu_custom_call" | custom-call | flops 805306368 | bytes 1572864 | tf_op jit(solution)/shard_map/layer_items/pallas_call | solution.py:333
  39.6 1.0 %collective-permute-start.11 = (bf16[2,2,128,128]{3,2,1,0:T(8,128)(2,1)S(1)}, bf16[2,2,128,128]{3,2,1,0:T(8,128)(2,1)S(1)}, u32[]{:S(2)}, u32[]{:S(2)}) collective-permute-start(bf16[2,2,128,128]{3,2,1,0:T(8,128)(2,1)S(1)} %get-tuple-element.45), channel_id=1, source_target_pairs={{0,4},{1,5},{2,6},{3,7},{4,0},{5,1},{6,2},{7,3},{8,12},{9,13},{10,... | collective-permute-start | bytes 393224 | tf_op jit(solution)/shard_map/ppermute | solution.py:34
  40.7 1.4 %collective-permute-start.14 = (bf16[2,2,128,128]{3,2,1,0:T(8,128)(2,1)S(1)}, bf16[2,2,128,128]{3,2,1,0:T(8,128)(2,1)S(1)}, u32[]{:S(2)}, u32[]{:S(2)}) collective-permute-start(bf16[2,2,128,128]{3,2,1,0:T(8,128)(2,1)S(1)} %get-tuple-element.47), channel_id=1, source_target_pairs={{0,2},{1,3},{2,0},{3,1},{4,6},{5,7},{6,4},{7,5},{8,10},{9,11},{10,... | collective-permute-start | bytes 393224 | tf_op jit(solution)/shard_map/ppermute | solution.py:34
  42.1 1.3 %collective-permute-start.16 = (bf16[2,2,128,128]{3,2,1,0:T(8,128)(2,1)S(1)}, bf16[2,2,128,128]{3,2,1,0:T(8,128)(2,1)S(1)}, u32[]{:S(2)}, u32[]{:S(2)}) collective-permute-start(bf16[2,2,128,128]{3,2,1,0:T(8,128)(2,1)S(1)} %get-tuple-element.51), channel_id=1, source_target_pairs={{0,4},{1,5},{2,6},{3,7},{4,0},{5,1},{6,2},{7,3},{8,12},{9,13},{10,... | collective-permute-start | bytes 393224 | tf_op jit(solution)/shard_map/ppermute | solution.py:34
  43.7 3.4 %mixed_perambulators.1.refs_8_ = bf16[2,4,2,128,512]{4,3,2,1,0:T(8,128)(2,1)S(1)} custom-call(s32[2]{0:T(128)S(1)} %get-tuple-element.56.slot_ref, s32[2]{0:T(128)S(1)} %get-tuple-element.55.structure_ref, f32[256]{0:T(256)S(1)} %reshape.17.weight_ref, bf16[2,4,2,128,512]{4,3,2,1,0:T(8,128)(2,1)} %tau_ref.1), custom_call_target="tpu_custom_call" | custom-call | flops 8388608 | bytes 4194304 | tf_op jit(solution)/shard_map/mixed_perambulators/pallas_call | solution.py:430
  47.1 3.9 %collective-permute-start.9 = (bf16[1,2,128,128]{3,2,1,0:T(8,128)(2,1)S(1)}, bf16[1,2,128,128]{3,2,1,0:T(8,128)(2,1)S(1)}, u32[]{:S(2)}, u32[]{:S(2)}) collective-permute-start(bf16[1,2,128,128]{3,2,1,0:T(8,128)(2,1)S(1)} %added.11), channel_id=1, source_target_pairs={{0,12},{1,13},{2,14},{3,15},{4,8},{5,9},{6,10},{7,11},{8,4},{9,5},... | collective-permute-start | bytes 196616 | tf_op jit(solution)/shard_map/ppermute | solution.py:34
  51.1 3.9 %collective-permute-start.12 = (bf16[1,2,128,128]{3,2,1,0:T(8,128)(2,1)S(1)}, bf16[1,2,128,128]{3,2,1,0:T(8,128)(2,1)S(1)}, u32[]{:S(2)}, u32[]{:S(2)}) collective-permute-start(bf16[1,2,128,128]{3,2,1,0:T(8,128)(2,1)S(1)} %added.14), channel_id=1, source_target_pairs={{0,10},{1,11},{2,8},{3,9},{4,14},{5,15},{6,12},{7,13},{8,2},{9,3},... | collective-permute-start | bytes 196616 | tf_op jit(solution)/shard_map/ppermute | solution.py:34
  55.2 0.6 collective-permute-start.15
  55.8 0.6 collective-permute-start.17
  56.4 1.0 %collective-permute-done.10.refs_1_ = bf16[1,2,128,128]{3,2,1,0:T(8,128)(2,1)S(1)} collective-permute-done((bf16[1,2,128,128]{3,2,1,0:T(8,128)(2,1)S(1)}, bf16[1,2,128,128]{3,2,1,0:T(8,128)(2,1)S(1)}, u32[]{:S(2)}, u32[]{:S(2)}) %collective-permute-start.10) | collective-permute-done | bytes 65568 | tf_op jit(solution)/shard_map/ppermute | solution.py:34
  57.4 3.4 %collective-permute-done.12.refs_2_ = bf16[1,2,128,128]{3,2,1,0:T(8,128)(2,1)S(1)} collective-permute-done((bf16[1,2,128,128]{3,2,1,0:T(8,128)(2,1)S(1)}, bf16[1,2,128,128]{3,2,1,0:T(8,128)(2,1)S(1)}, u32[]{:S(2)}, u32[]{:S(2)}) %collective-permute-start.12) | collective-permute-done | bytes 65568 | tf_op jit(solution)/shard_map/ppermute | solution.py:34
  60.9 0.6 collective-permute-done.15.refs_4_
  61.4 1.6 %diagrams.1 = bf16[2,4,2,128,512]{4,3,2,1,0:T(8,128)(2,1)} custom-call(bf16[1,2,128,128]{3,2,1,0:T(8,128)(2,1)S(1)} %collective-permute-done.9.refs_0_, bf16[1,2,128,128]{3,2,1,0:T(8,128)(2,1)S(1)} %collective-permute-done.10.refs_1_, bf16[1,2,128,128]{3,2,1,0:T(8,128)(2,1)S(1)} %collective-permute-done.12.refs_2_, ...), custom_call_target="tpu_custom_call" | custom-call | flops 536870912 | bytes 4194304 | tf_op jit(solution)/shard_map/diagrams/pallas_call | solution.py:477
  (43 shorter events, 2.2 us)
Async XLA Ops:
  0.0 3.1 %collective-permute-start = (s32[1,2,3]{2,1,0:T(2,128)}, s32[1,2,3]{2,1,0:T(2,128)S(1)}, u32[]{:S(2)}, u32[]{:S(2)}) collective-permute-start(s32[1,2,3]{2,1,0:T(2,128)} %bitcast.7), channel_id=1, source_target_pairs={{0,1},{1,0},{2,3},{3,2},{4,5},{5,4},{6,7},{7,6},{8,9},{9,8},{10,11... | collective-permute-start | bytes 80 | tf_op jit(solution)/shard_map/ppermute | solution.py:34
  0.5 4.3 %collective-permute-start.1 = (s32[1,2,3]{2,1,0:T(2,128)}, s32[1,2,3]{2,1,0:T(2,128)S(1)}, u32[]{:S(2)}, u32[]{:S(2)}) collective-permute-start(s32[1,2,3]{2,1,0:T(2,128)} %bitcast.8), channel_id=1, source_target_pairs={{0,2},{1,3},{2,0},{3,1},{4,6},{5,7},{6,4},{7,5},{8,10},{9,11},{10,... | collective-permute-start | bytes 80 | tf_op jit(solution)/shard_map/ppermute | solution.py:34
  3.0 3.2 %collective-permute-start.2 = (s32[1,2,3]{2,1,0:T(2,128)}, s32[1,2,3]{2,1,0:T(2,128)S(1)}, u32[]{:S(2)}, u32[]{:S(2)}) collective-permute-start(s32[1,2,3]{2,1,0:T(2,128)} %bitcast.9), channel_id=1, source_target_pairs={{0,3},{1,2},{2,1},{3,0},{4,7},{5,6},{6,5},{7,4},{8,11},{9,10},{10,... | collective-permute-start | bytes 80 | tf_op jit(solution)/shard_map/ppermute | solution.py:34
  6.2 23.4 %collective-permute-start.6 = (bf16[4,2,3,128,1,256]{5,3,2,1,0,4:T(8,128)(2,1)}, bf16[4,2,3,128,1,256]{5,3,2,1,0,4:T(8,128)(2,1)S(1)}, u32[]{:S(2)}, u32[]{:S(2)}) collective-permute-start(bf16[4,2,3,128,1,256]{5,3,2,1,0,4:T(8,128)(2,1)} %bitcast.11), channel_id=1, source_target_pairs={{0,15},{1,0},{2,1},{3,2},{4,3},{5,4},{6,5},{7,6},{8,7},{9,8},{10,9... | collective-permute-start | bytes 4718600 | tf_op jit(solution)/shard_map/ppermute | solution.py:25
  10.2 19.3 %collective-permute-start.3 = (s32[4,2,3]{2,1,0:T(2,128)S(1)}, s32[4,2,3]{2,1,0:T(2,128)S(1)}, u32[]{:S(2)}, u32[]{:S(2)}) collective-permute-start(s32[4,2,3]{2,1,0:T(2,128)S(1)} %pad_add_fusion), channel_id=1, source_target_pairs={{0,4},{1,5},{2,6},{3,7},{4,0},{5,1},{6,2},{7,3},{8,12},{9,13},{10,... | collective-permute-start | bytes 296 | tf_op jit(solution)/shard_map/ppermute | solution.py:34
  10.2 19.3 %collective-permute-start.4 = (s32[4,2,3]{2,1,0:T(2,128)S(1)}, s32[4,2,3]{2,1,0:T(2,128)S(1)}, u32[]{:S(2)}, u32[]{:S(2)}) collective-permute-start(s32[4,2,3]{2,1,0:T(2,128)S(1)} %pad_add_fusion), channel_id=1, source_target_pairs={{0,8},{1,9},{2,10},{3,11},{4,12},{5,13},{6,14},{7,15},{8,0},{9,1},... | collective-permute-start | bytes 296 | tf_op jit(solution)/shard_map/ppermute | solution.py:34
  11.3 18.3 %collective-permute-start.5 = (s32[4,2,3]{2,1,0:T(2,128)S(1)}, s32[4,2,3]{2,1,0:T(2,128)S(1)}, u32[]{:S(2)}, u32[]{:S(2)}) collective-permute-start(s32[4,2,3]{2,1,0:T(2,128)S(1)} %pad_add_fusion), channel_id=1, source_target_pairs={{0,12},{1,13},{2,14},{3,15},{4,8},{5,9},{6,10},{7,11},{8,4},{9,5},... | collective-permute-start | bytes 296 | tf_op jit(solution)/shard_map/ppermute | solution.py:34
  32.1 1.1 %copy-start = (bf16[4,2,3,128,1,256]{5,3,2,1,0,4:T(8,128)(2,1)}, bf16[4,2,3,128,1,256]{5,3,2,1,0,4:T(8,128)(2,1)S(1)}, u32[]{:S(2)}) copy-start(bf16[4,2,3,128,1,256]{5,3,2,1,0,4:T(8,128)(2,1)S(1)} %collective-permute-done.6) | copy-start | bytes 4718596
  33.2 5.4 %collective-permute-start.7 = (bf16[16,2,128,128]{3,2,1,0:T(8,128)(2,1)S(1)}, bf16[16,2,128,128]{3,2,1,0:T(8,128)(2,1)S(1)}, u32[]{:S(2)}, u32[]{:S(2)}) collective-permute-start(bf16[16,2,128,128]{3,2,1,0:T(8,128)(2,1)S(1)} %layer_items.3), channel_id=1, source_target_pairs={{0,1},{1,0},{2,3},{3,2},{4,5},{5,4},{6,7},{7,6},{8,9},{9,8},{10,11... | collective-permute-start | bytes 3145736 | tf_op jit(solution)/shard_map/ppermute | solution.py:34
  33.2 1.4 %copy-start.1 = (bf16[4,2,3,128,1,256]{5,3,2,1,0,4:T(8,128)(2,1)S(1)}, bf16[4,2,3,128,1,256]{5,3,2,1,0,4:T(8,128)(2,1)}, u32[]{:S(2)}) copy-start(bf16[4,2,3,128,1,256]{5,3,2,1,0,4:T(8,128)(2,1)} %copy-done) | copy-start | bytes 4718596
  38.6 0.7 %copy-start.3 = (f32[16,4,4]{0,2,1:T(4,128)S(1)}, f32[16,4,4]{0,2,1:T(4,128)}, u32[]{:S(2)}) copy-start(f32[16,4,4]{0,2,1:T(4,128)} %param.9) | copy-start | bytes 3076
  38.7 8.3 %collective-permute-start.8 = (bf16[2,2,128,128]{3,2,1,0:T(8,128)(2,1)S(1)}, bf16[2,2,128,128]{3,2,1,0:T(8,128)(2,1)S(1)}, u32[]{:S(2)}, u32[]{:S(2)}) collective-permute-start(bf16[2,2,128,128]{3,2,1,0:T(8,128)(2,1)S(1)} %get-tuple-element.41), channel_id=1, source_target_pairs={{0,2},{1,3},{2,0},{3,1},{4,6},{5,7},{6,4},{7,5},{8,10},{9,11},{10,... | collective-permute-start | bytes 393224 | tf_op jit(solution)/shard_map/ppermute | solution.py:34
  39.6 3.8 %copy-start.2 = (s32[2,3]{1,0:T(2,128)S(1)}, s32[2,3]{1,0:T(2,128)}, u32[]{:S(2)}) copy-start(s32[2,3]{1,0:T(2,128)} %param.11) | copy-start | bytes 76
  39.6 11.5 %collective-permute-start.11 = (bf16[2,2,128,128]{3,2,1,0:T(8,128)(2,1)S(1)}, bf16[2,2,128,128]{3,2,1,0:T(8,128)(2,1)S(1)}, u32[]{:S(2)}, u32[]{:S(2)}) collective-permute-start(bf16[2,2,128,128]{3,2,1,0:T(8,128)(2,1)S(1)} %get-tuple-element.45), channel_id=1, source_target_pairs={{0,4},{1,5},{2,6},{3,7},{4,0},{5,1},{6,2},{7,3},{8,12},{9,13},{10,... | collective-permute-start | bytes 393224 | tf_op jit(solution)/shard_map/ppermute | solution.py:34
  40.7 14.3 %collective-permute-start.14 = (bf16[2,2,128,128]{3,2,1,0:T(8,128)(2,1)S(1)}, bf16[2,2,128,128]{3,2,1,0:T(8,128)(2,1)S(1)}, u32[]{:S(2)}, u32[]{:S(2)}) collective-permute-start(bf16[2,2,128,128]{3,2,1,0:T(8,128)(2,1)S(1)} %get-tuple-element.47), channel_id=1, source_target_pairs={{0,2},{1,3},{2,0},{3,1},{4,6},{5,7},{6,4},{7,5},{8,10},{9,11},{10,... | collective-permute-start | bytes 393224 | tf_op jit(solution)/shard_map/ppermute | solution.py:34
  42.1 13.0 %collective-permute-start.16 = (bf16[2,2,128,128]{3,2,1,0:T(8,128)(2,1)S(1)}, bf16[2,2,128,128]{3,2,1,0:T(8,128)(2,1)S(1)}, u32[]{:S(2)}, u32[]{:S(2)}) collective-permute-start(bf16[2,2,128,128]{3,2,1,0:T(8,128)(2,1)S(1)} %get-tuple-element.51), channel_id=1, source_target_pairs={{0,4},{1,5},{2,6},{3,7},{4,0},{5,1},{6,2},{7,3},{8,12},{9,13},{10,... | collective-permute-start | bytes 393224 | tf_op jit(solution)/shard_map/ppermute | solution.py:34
  47.1 8.7 %collective-permute-start.9 = (bf16[1,2,128,128]{3,2,1,0:T(8,128)(2,1)S(1)}, bf16[1,2,128,128]{3,2,1,0:T(8,128)(2,1)S(1)}, u32[]{:S(2)}, u32[]{:S(2)}) collective-permute-start(bf16[1,2,128,128]{3,2,1,0:T(8,128)(2,1)S(1)} %added.11), channel_id=1, source_target_pairs={{0,12},{1,13},{2,14},{3,15},{4,8},{5,9},{6,10},{7,11},{8,4},{9,5},... | collective-permute-start | bytes 196616 | tf_op jit(solution)/shard_map/ppermute | solution.py:34
  51.0 6.4 %collective-permute-start.10 = (bf16[1,2,128,128]{3,2,1,0:T(8,128)(2,1)S(1)}, bf16[1,2,128,128]{3,2,1,0:T(8,128)(2,1)S(1)}, u32[]{:S(2)}, u32[]{:S(2)}) collective-permute-start(bf16[1,2,128,128]{3,2,1,0:T(8,128)(2,1)S(1)} %added.12), channel_id=1, source_target_pairs={{0,8},{1,9},{2,10},{3,11},{4,12},{5,13},{6,14},{7,15},{8,0},{9,1},... | collective-permute-start | bytes 196616 | tf_op jit(solution)/shard_map/ppermute | solution.py:34
  51.1 9.7 %collective-permute-start.12 = (bf16[1,2,128,128]{3,2,1,0:T(8,128)(2,1)S(1)}, bf16[1,2,128,128]{3,2,1,0:T(8,128)(2,1)S(1)}, u32[]{:S(2)}, u32[]{:S(2)}) collective-permute-start(bf16[1,2,128,128]{3,2,1,0:T(8,128)(2,1)S(1)} %added.14), channel_id=1, source_target_pairs={{0,10},{1,11},{2,8},{3,9},{4,14},{5,15},{6,12},{7,13},{8,2},{9,3},... | collective-permute-start | bytes 196616 | tf_op jit(solution)/shard_map/ppermute | solution.py:34
  55.0 5.8 %collective-permute-start.13 = (bf16[1,2,128,128]{3,2,1,0:T(8,128)(2,1)S(1)}, bf16[1,2,128,128]{3,2,1,0:T(8,128)(2,1)S(1)}, u32[]{:S(2)}, u32[]{:S(2)}) collective-permute-start(bf16[1,2,128,128]{3,2,1,0:T(8,128)(2,1)S(1)} %added.15), channel_id=1, source_target_pairs={{0,8},{1,9},{2,10},{3,11},{4,12},{5,13},{6,14},{7,15},{8,0},{9,1},... | collective-permute-start | bytes 196616 | tf_op jit(solution)/shard_map/ppermute | solution.py:34
  55.2 6.3 %collective-permute-start.15 = (bf16[1,2,128,128]{3,2,1,0:T(8,128)(2,1)S(1)}, bf16[1,2,128,128]{3,2,1,0:T(8,128)(2,1)S(1)}, u32[]{:S(2)}, u32[]{:S(2)}) collective-permute-start(bf16[1,2,128,128]{3,2,1,0:T(8,128)(2,1)S(1)} %get-tuple-element.48), channel_id=1, source_target_pairs={{0,4},{1,5},{2,6},{3,7},{4,0},{5,1},{6,2},{7,3},{8,12},{9,13},{10,... | collective-permute-start | bytes 196616 | tf_op jit(solution)/shard_map/ppermute | solution.py:34
  55.8 5.6 %collective-permute-start.17 = (bf16[1,2,128,128]{3,2,1,0:T(8,128)(2,1)S(1)}, bf16[1,2,128,128]{3,2,1,0:T(8,128)(2,1)S(1)}, u32[]{:S(2)}, u32[]{:S(2)}) collective-permute-start(bf16[1,2,128,128]{3,2,1,0:T(8,128)(2,1)S(1)} %get-tuple-element.52), channel_id=1, source_target_pairs={{0,2},{1,3},{2,0},{3,1},{4,6},{5,7},{6,4},{7,5},{8,10},{9,11},{10,... | collective-permute-start | bytes 196616 | tf_op jit(solution)/shard_map/ppermute | solution.py:34
where the time goes:
time: 63.4 us; the launch traced here: 63 us
  Pallas kernels  26.7 us (42%)
  starting transfers between devices  23.8 us (38%)
  waiting for transfers between devices  8.07 us (13%)
  local copies, waits for them, and re-layouts  3.33 us (5%)
  other arithmetic  0.9 us (1%)
    ppermute x17, starting transfers between devices, exchanged(): return lax.ppermute(value, SITES, [(i, i ^ mask) for i in range(size)])  20.5 us
    pallas_call x1, Pallas kernels, plane_items(): pl.pallas_call(functools.partial(plane_kernel, total_z, plane, scale), gr...  14.9 us
    ppermute x17, waiting for transfers between devices, exchanged(): return lax.ppermute(value, SITES, [(i, i ^ mask) for i in range(size)])  8.07 us
    pallas_call x2, Pallas kernels, layer_items(): pl.pallas_call(functools.partial(layer_kernel, core, scale), in_specs=[pl...  6.44 us
    pallas_call x1, Pallas kernels, mixed_perambulators(): pl.pallas_call(mix_kernel, grid_spec=pltpu.PrefetchScalarGridSpec(num_sca...  3.38 us
    ppermute x1, starting transfers between devices, shifted(): lax.ppermute(value, axis, [(i, (i + by) % size) for i in range(size)])  3.38 us
    unnamed x12, local copies, waits for them, and re-layouts  3.21 us
    pallas_call x1, Pallas kernels, diagrams(): pl.pallas_call(functools.partial(diagram_kernel, owners), in_specs=[whole...  1.61 us
  transfers between devices with their start and end apart: 18, of which 5 were waited for; matrix products, arithmetic and copies ran while one was open for 2% of the time, Pallas kernels for 36%

commit v1 on v0

--- a/solution.py
+++ b/solution.py
@@ -17,7 +17,7 @@
 ROWS = 16
 SITES = ("space", "diag")
 MIB = 1024 * 1024
-PLANE_LIMIT = 24 * MIB
+PLANE_LIMIT = 20 * MIB
 
 
 def shifted(value, axis, by):
@@ -339,7 +339,7 @@
             pltpu.VMEM((2, 4 * nvec, NCOL * width), jnp.bfloat16),
             pltpu.SMEM((total,), jnp.int32),
         ],
-        compiler_params=pltpu.CompilerParams(vmem_limit_bytes=12 * MIB),
+        compiler_params=pltpu.CompilerParams(vmem_limit_bytes=8 * MIB),
         cost_estimate=pl.CostEstimate(
             flops=total * 4 * nvec * nvec * NCOL * width,
             bytes_accessed=2 * own.size,
@@ -483,7 +483,7 @@
             pltpu.VMEM(tau.shape, jnp.bfloat16),
             pltpu.SemaphoreType.DMA((count, spins)),
         ],
-        compiler_params=pltpu.CompilerParams(vmem_limit_bytes=12 * MIB),
+        compiler_params=pltpu.CompilerParams(vmem_limit_bytes=8 * MIB),
         cost_estimate=pl.CostEstimate(
             flops=8 * nvec * nvec * width * spins * count, bytes_accessed=4 * tau.size, transcendentals=0
         ),
@@ -518,9 +518,6 @@
     ]
     chunks = list(zip(*[[chunks[slot][half]() for slot in slots] for half in range(2)]))
     chunks = [list(pair) for pair in chunks]
-    first = chunks[0][0]
-    values, tau = lax.optimization_barrier(([value for _, value in first], tau))
-    chunks[0][0] = [(left, value) for (left, _), value in zip(first, values)]
     owners = []
     parts = []
     for half in range(2):

time: 63.4 us -> 58.4 us (0.921)
  local copies, waits for them, and re-layouts: 3.33 us -> 0.26 us
  waiting for transfers between devices: 8.07 us -> 6.49 us
  Pallas kernels: 26.7 us -> 25.9 us
    unnamed x12 -> x8, local copies, waits for them, and re-layouts: 3.21 us -> 0.14 us
    ppermute x17, waiting for transfers between devices: 8.07 us -> 6.48 us  [exchanged(): return lax.ppermute(value, SITES, [(i, i ^ mask) for i in range(size)])]
    pallas_call x2, Pallas kernels: 6.44 us -> 5.68 us  [layer_items(): pl.pallas_call(functools.partial(layer_kernel, core, scale), in_specs=[pl...]
  transfers between devices with their start and end apart: 18 -> 18, of which waited for: 5 -> 5; matrix products, arithmetic and copies ran while one was open for 2% -> 2% of each run, Pallas kernels for 36% -> 37%
where the time goes in v1:
time: 58.4 us; the launch traced here: 58.2 us
  Pallas kernels  25.9 us (44%)
  starting transfers between devices  24.4 us (42%)
  waiting for transfers between devices  6.49 us (11%)
  other arithmetic  0.9 us (2%)
    ppermute x17, starting transfers between devices, exchanged(): return lax.ppermute(value, SITES, [(i, i ^ mask) for i in range(size)])  21 us
    pallas_call x1, Pallas kernels, plane_items(): pl.pallas_call(functools.partial(plane_kernel, total_z, plane, scale), gr...  14.9 us
    ppermute x17, waiting for transfers between devices, exchanged(): return lax.ppermute(value, SITES, [(i, i ^ mask) for i in range(size)])  6.48 us
    pallas_call x2, Pallas kernels, layer_items(): pl.pallas_call(functools.partial(layer_kernel, core, scale), in_specs=[pl...  5.68 us
    pallas_call x1, Pallas kernels, mixed_perambulators(): pl.pallas_call(mix_kernel, grid_spec=pltpu.PrefetchScalarGridSpec(num_sca...  3.38 us
    ppermute x1, starting transfers between devices, shifted(): lax.ppermute(value, axis, [(i, (i + by) % size) for i in range(size)])  3.38 us
    pallas_call x1, Pallas kernels, diagrams(): pl.pallas_call(functools.partial(diagram_kernel, owners), in_specs=[whole...  1.61 us
  transfers between devices with their start and end apart: 18, of which 5 were waited for; matrix products, arithmetic and copies ran while one was open for 2% of the time, Pallas kernels for 37%

profile of v1, /device:TPU:0, one launch (start us, length us, event | category | flops | bytes accessed | tf_op | source)
XLA Modules:
  0.0 58.2 jit_solution(9579609424129964984)
XLA Ops:
  0.0 0.5 collective-permute-start
  0.5 2.5 %collective-permute-start.1 = (s32[1,2,3]{2,1,0:T(2,128)}, s32[1,2,3]{2,1,0:T(2,128)S(1)}, u32[]{:S(2)}, u32[]{:S(2)}) collective-permute-start(s32[1,2,3]{2,1,0:T(2,128)} %bitcast.8), channel_id=1, source_target_pairs={{0,2},{1,3},{2,0},{3,1},{4,6},{5,7},{6,4},{7,5},{8,10},{9,11},{10,... | collective-permute-start | bytes 80 | tf_op jit(solution)/shard_map/ppermute | solution.py:34
  3.1 1.6 %collective-permute-done.1 = s32[1,2,3]{2,1,0:T(2,128)S(1)} collective-permute-done((s32[1,2,3]{2,1,0:T(2,128)}, s32[1,2,3]{2,1,0:T(2,128)S(1)}, u32[]{:S(2)}, u32[]{:S(2)}) %collective-permute-start.1) | collective-permute-done | bytes 56 | tf_op jit(solution)/shard_map/ppermute | solution.py:34
  4.7 1.4 %collective-permute-done.2 = s32[1,2,3]{2,1,0:T(2,128)S(1)} collective-permute-done((s32[1,2,3]{2,1,0:T(2,128)}, s32[1,2,3]{2,1,0:T(2,128)S(1)}, u32[]{:S(2)}, u32[]{:S(2)}) %collective-permute-start.2) | collective-permute-done | bytes 56 | tf_op jit(solution)/shard_map/ppermute | solution.py:34
  6.2 3.4 %collective-permute-start.6 = (bf16[4,2,3,128,1,256]{5,3,2,1,0,4:T(8,128)(2,1)}, bf16[4,2,3,128,1,256]{5,3,2,1,0,4:T(8,128)(2,1)S(1)}, u32[]{:S(2)}, u32[]{:S(2)}) collective-permute-start(bf16[4,2,3,128,1,256]{5,3,2,1,0,4:T(8,128)(2,1)} %bitcast.11), channel_id=1, source_target_pairs={{0,15},{1,0},{2,1},{3,2},{4,3},{5,4},{6,5},{7,6},{8,7},{9,8},{10,9... | collective-permute-start | bytes 4718600 | tf_op jit(solution)/shard_map/ppermute | solution.py:25
  9.6 0.7 %pad_add_fusion = s32[4,2,3]{2,1,0:T(2,128)S(1)} fusion(s32[1,2,3]{2,1,0:T(2,128)S(1)} %collective-permute-done.2, s32[1,2,3]{2,1,0:T(2,128)S(1)} %collective-permute-done.1, s32[1,2,3]{2,1,0:T(2,128)S(1)} %collective-permute-done, s32[1,2,3]{2,1,0:T(2,128)} %bitcast.10), kind=kLoop, calls=%fused_computation.4 | loop fusion | flops 72 | bytes 192 | tf_op jit(solution)/shard_map/concatenate | solution.py:46
  10.2 1.0 %collective-permute-start.4 = (s32[4,2,3]{2,1,0:T(2,128)S(1)}, s32[4,2,3]{2,1,0:T(2,128)S(1)}, u32[]{:S(2)}, u32[]{:S(2)}) collective-permute-start(s32[4,2,3]{2,1,0:T(2,128)S(1)} %pad_add_fusion), channel_id=1, source_target_pairs={{0,8},{1,9},{2,10},{3,11},{4,12},{5,13},{6,14},{7,15},{8,0},{9,1},... | collective-permute-start | bytes 296 | tf_op jit(solution)/shard_map/ppermute | solution.py:34
  11.3 3.4 %collective-permute-start.5 = (s32[4,2,3]{2,1,0:T(2,128)S(1)}, s32[4,2,3]{2,1,0:T(2,128)S(1)}, u32[]{:S(2)}, u32[]{:S(2)}) collective-permute-start(s32[4,2,3]{2,1,0:T(2,128)S(1)} %pad_add_fusion), channel_id=1, source_target_pairs={{0,12},{1,13},{2,14},{3,15},{4,8},{5,9},{6,10},{7,11},{8,4},{9,5},... | collective-permute-start | bytes 296 | tf_op jit(solution)/shard_map/ppermute | solution.py:34
  14.6 14.9 %plane_items.1 = (bf16[4,4,3,2,128,128]{5,4,3,2,1,0:T(8,128)(2,1)S(1)}, f32[4,2,3,128,256]{4,3,2,1,0:T(8,128)S(1)}, f32[4,2,1,256]{3,2,1,0:T(1,128)S(1)}, f32[4,2,1,128]{3,2,1,0:T(1,128)S(1)}) custom-call(s32[1]{0:T(128)} %bitcast.1.position_ref, s32[4,3]{1,0:T(4,128)} %momenta_in.1, bf16[4,2,3,128,256]{4,3,2,1,0:T(8,128)(2,1)} %bitcast.12, ...), custom_call_target="tpu_custom_call" | custom-call | flops 3221225472 | bytes 4939776 | tf_op jit(solution)/shard_map/plane_items/pallas_call | solution.py:226
  29.6 2.5 %layer_items.3 = bf16[16,2,128,128]{3,2,1,0:T(8,128)(2,1)S(1)} custom-call(s32[16,2,3]{2,1,0:T(2,128)S(1)} %constant_dynamic-update-slice_fusion.rows_ref, bf16[4,4,3,2,128,128]{5,4,3,2,1,0:T(8,128)(2,1)S(1)} %get-tuple-element.32.item_ref, f32[4,2,3,128,256]{4,3,2,1,0:T(8,128)S(1)} %get-tuple-element.33.own_ref, bf16[4,2,3,128,256]{4,3,2,1,0:T(8,128)(2,1)S(1)} %bitcast.5, ...), custom_call_target="tpu_custom_call" | custom-call | flops 805306368 | bytes 1572864 | tf_op jit(solution)/shard_map/layer_items/pallas_call | solution.py:333
  32.2 3.2 %layer_items.2.refs_0_ = bf16[16,2,128,128]{3,2,1,0:T(8,128)(2,1)S(1)} custom-call(s32[16,2,3]{2,1,0:T(2,128)S(1)} %constant_dynamic-update-slice_fusion.rows_ref, bf16[4,4,3,2,128,128]{5,4,3,2,1,0:T(8,128)(2,1)S(1)} %get-tuple-element.32.item_ref, f32[4,2,3,128,256]{4,3,2,1,0:T(8,128)S(1)} %get-tuple-element.33.own_ref, ...), custom_call_target="tpu_custom_call" | custom-call | flops 805306368 | bytes 1572864 | tf_op jit(solution)/shard_map/layer_items/pallas_call | solution.py:333
  35.6 0.8 %collective-permute-start.11 = (bf16[2,2,128,128]{3,2,1,0:T(8,128)(2,1)S(1)}, bf16[2,2,128,128]{3,2,1,0:T(8,128)(2,1)S(1)}, u32[]{:S(2)}, u32[]{:S(2)}) collective-permute-start(bf16[2,2,128,128]{3,2,1,0:T(8,128)(2,1)S(1)} %get-tuple-element.40), channel_id=1, source_target_pairs={{0,4},{1,5},{2,6},{3,7},{4,0},{5,1},{6,2},{7,3},{8,12},{9,13},{10,... | collective-permute-start | bytes 393224 | tf_op jit(solution)/shard_map/ppermute | solution.py:34
  36.5 2.1 %collective-permute-start.14 = (bf16[2,2,128,128]{3,2,1,0:T(8,128)(2,1)S(1)}, bf16[2,2,128,128]{3,2,1,0:T(8,128)(2,1)S(1)}, u32[]{:S(2)}, u32[]{:S(2)}) collective-permute-start(bf16[2,2,128,128]{3,2,1,0:T(8,128)(2,1)S(1)} %get-tuple-element.42), channel_id=1, source_target_pairs={{0,2},{1,3},{2,0},{3,1},{4,6},{5,7},{6,4},{7,5},{8,10},{9,11},{10,... | collective-permute-start | bytes 393224 | tf_op jit(solution)/shard_map/ppermute | solution.py:34
  38.7 1.3 %collective-permute-start.16 = (bf16[2,2,128,128]{3,2,1,0:T(8,128)(2,1)S(1)}, bf16[2,2,128,128]{3,2,1,0:T(8,128)(2,1)S(1)}, u32[]{:S(2)}, u32[]{:S(2)}) collective-permute-start(bf16[2,2,128,128]{3,2,1,0:T(8,128)(2,1)S(1)} %get-tuple-element.46), channel_id=1, source_target_pairs={{0,4},{1,5},{2,6},{3,7},{4,0},{5,1},{6,2},{7,3},{8,12},{9,13},{10,... | collective-permute-start | bytes 393224 | tf_op jit(solution)/shard_map/ppermute | solution.py:34
  40.0 1.9 %collective-permute-done.8.refs_1_ = bf16[2,2,128,128]{3,2,1,0:T(8,128)(2,1)S(1)} collective-permute-done((bf16[2,2,128,128]{3,2,1,0:T(8,128)(2,1)S(1)}, bf16[2,2,128,128]{3,2,1,0:T(8,128)(2,1)S(1)}, u32[]{:S(2)}, u32[]{:S(2)}) %collective-permute-start.8) | collective-permute-done | bytes 131104 | tf_op jit(solution)/shard_map/ppermute | solution.py:34
  42.0 2.6 %collective-permute-start.9 = (bf16[1,2,128,128]{3,2,1,0:T(8,128)(2,1)S(1)}, bf16[1,2,128,128]{3,2,1,0:T(8,128)(2,1)S(1)}, u32[]{:S(2)}, u32[]{:S(2)}) collective-permute-start(bf16[1,2,128,128]{3,2,1,0:T(8,128)(2,1)S(1)} %added.11), channel_id=1, source_target_pairs={{0,12},{1,13},{2,14},{3,15},{4,8},{5,9},{6,10},{7,11},{8,4},{9,5},... | collective-permute-start | bytes 196616 | tf_op jit(solution)/shard_map/ppermute | solution.py:34
  44.9 4.2 %collective-permute-start.12 = (bf16[1,2,128,128]{3,2,1,0:T(8,128)(2,1)S(1)}, bf16[1,2,128,128]{3,2,1,0:T(8,128)(2,1)S(1)}, u32[]{:S(2)}, u32[]{:S(2)}) collective-permute-start(bf16[1,2,128,128]{3,2,1,0:T(8,128)(2,1)S(1)} %added.14), channel_id=1, source_target_pairs={{0,10},{1,11},{2,8},{3,9},{4,14},{5,15},{6,12},{7,13},{8,2},{9,3},... | collective-permute-start | bytes 196616 | tf_op jit(solution)/shard_map/ppermute | solution.py:34
  49.3 0.6 %collective-permute-start.15 = (bf16[1,2,128,128]{3,2,1,0:T(8,128)(2,1)S(1)}, bf16[1,2,128,128]{3,2,1,0:T(8,128)(2,1)S(1)}, u32[]{:S(2)}, u32[]{:S(2)}) collective-permute-start(bf16[1,2,128,128]{3,2,1,0:T(8,128)(2,1)S(1)} %get-tuple-element.43), channel_id=1, source_target_pairs={{0,4},{1,5},{2,6},{3,7},{4,0},{5,1},{6,2},{7,3},{8,12},{9,13},{10,... | collective-permute-start | bytes 196616 | tf_op jit(solution)/shard_map/ppermute | solution.py:34
  50.0 1.5 %collective-permute-start.17 = (bf16[1,2,128,128]{3,2,1,0:T(8,128)(2,1)S(1)}, bf16[1,2,128,128]{3,2,1,0:T(8,128)(2,1)S(1)}, u32[]{:S(2)}, u32[]{:S(2)}) collective-permute-start(bf16[1,2,128,128]{3,2,1,0:T(8,128)(2,1)S(1)} %get-tuple-element.47), channel_id=1, source_target_pairs={{0,2},{1,3},{2,0},{3,1},{4,6},{5,7},{6,4},{7,5},{8,10},{9,11},{10,... | collective-permute-start | bytes 196616 | tf_op jit(solution)/shard_map/ppermute | solution.py:34
  51.5 0.2 slice_reduce_fusion
  51.7 3.4 %mixed_perambulators.1.refs_8_ = bf16[2,4,2,128,512]{4,3,2,1,0:T(8,128)(2,1)S(1)} custom-call(s32[2]{0:T(128)S(1)} %get-tuple-element.50.slot_ref, s32[2]{0:T(128)S(1)} %get-tuple-element.49.structure_ref, f32[256]{0:T(256)S(1)} %reshape.17.weight_ref, bf16[2,4,2,128,512]{4,3,2,1,0:T(8,128)(2,1)} %tau_ref.1), custom_call_target="tpu_custom_call" | custom-call | flops 8388608 | bytes 4194304 | tf_op jit(solution)/shard_map/mixed_perambulators/pallas_call | solution.py:430
  55.1 0.9 %collective-permute-done.13.refs_3_ = bf16[1,2,128,128]{3,2,1,0:T(8,128)(2,1)S(1)} collective-permute-done((bf16[1,2,128,128]{3,2,1,0:T(8,128)(2,1)S(1)}, bf16[1,2,128,128]{3,2,1,0:T(8,128)(2,1)S(1)}, u32[]{:S(2)}, u32[]{:S(2)}) %collective-permute-start.13) | collective-permute-done | bytes 65568 | tf_op jit(solution)/shard_map/ppermute | solution.py:34
  56.0 0.6 %collective-permute-done.15.refs_4_ = bf16[1,2,128,128]{3,2,1,0:T(8,128)(2,1)S(1)} collective-permute-done((bf16[1,2,128,128]{3,2,1,0:T(8,128)(2,1)S(1)}, bf16[1,2,128,128]{3,2,1,0:T(8,128)(2,1)S(1)}, u32[]{:S(2)}, u32[]{:S(2)}) %collective-permute-start.15) | collective-permute-done | bytes 65568 | tf_op jit(solution)/shard_map/ppermute | solution.py:34
  56.6 1.6 %diagrams.1 = bf16[2,4,2,128,512]{4,3,2,1,0:T(8,128)(2,1)} custom-call(bf16[1,2,128,128]{3,2,1,0:T(8,128)(2,1)S(1)} %collective-permute-done.9.refs_0_, bf16[1,2,128,128]{3,2,1,0:T(8,128)(2,1)S(1)} %collective-permute-done.10.refs_1_, bf16[1,2,128,128]{3,2,1,0:T(8,128)(2,1)S(1)} %collective-permute-done.12.refs_2_, ...), custom_call_target="tpu_custom_call" | custom-call | flops 536870912 | bytes 4194304 | tf_op jit(solution)/shard_map/diagrams/pallas_call | solution.py:477
  (39 shorter events, 1.1 us)
Async XLA Ops:
  0.0 3.1 %collective-permute-start = (s32[1,2,3]{2,1,0:T(2,128)}, s32[1,2,3]{2,1,0:T(2,128)S(1)}, u32[]{:S(2)}, u32[]{:S(2)}) collective-permute-start(s32[1,2,3]{2,1,0:T(2,128)} %bitcast.7), channel_id=1, source_target_pairs={{0,1},{1,0},{2,3},{3,2},{4,5},{5,4},{6,7},{7,6},{8,9},{9,8},{10,11... | collective-permute-start | bytes 80 | tf_op jit(solution)/shard_map/ppermute | solution.py:34
  0.5 4.3 %collective-permute-start.1 = (s32[1,2,3]{2,1,0:T(2,128)}, s32[1,2,3]{2,1,0:T(2,128)S(1)}, u32[]{:S(2)}, u32[]{:S(2)}) collective-permute-start(s32[1,2,3]{2,1,0:T(2,128)} %bitcast.8), channel_id=1, source_target_pairs={{0,2},{1,3},{2,0},{3,1},{4,6},{5,7},{6,4},{7,5},{8,10},{9,11},{10,... | collective-permute-start | bytes 80 | tf_op jit(solution)/shard_map/ppermute | solution.py:34
  3.0 3.2 %collective-permute-start.2 = (s32[1,2,3]{2,1,0:T(2,128)}, s32[1,2,3]{2,1,0:T(2,128)S(1)}, u32[]{:S(2)}, u32[]{:S(2)}) collective-permute-start(s32[1,2,3]{2,1,0:T(2,128)} %bitcast.9), channel_id=1, source_target_pairs={{0,3},{1,2},{2,1},{3,0},{4,7},{5,6},{6,5},{7,4},{8,11},{9,10},{10,... | collective-permute-start | bytes 80 | tf_op jit(solution)/shard_map/ppermute | solution.py:34
  6.2 23.4 %collective-permute-start.6 = (bf16[4,2,3,128,1,256]{5,3,2,1,0,4:T(8,128)(2,1)}, bf16[4,2,3,128,1,256]{5,3,2,1,0,4:T(8,128)(2,1)S(1)}, u32[]{:S(2)}, u32[]{:S(2)}) collective-permute-start(bf16[4,2,3,128,1,256]{5,3,2,1,0,4:T(8,128)(2,1)} %bitcast.11), channel_id=1, source_target_pairs={{0,15},{1,0},{2,1},{3,2},{4,3},{5,4},{6,5},{7,6},{8,7},{9,8},{10,9... | collective-permute-start | bytes 4718600 | tf_op jit(solution)/shard_map/ppermute | solution.py:25
  10.2 19.3 %collective-permute-start.3 = (s32[4,2,3]{2,1,0:T(2,128)S(1)}, s32[4,2,3]{2,1,0:T(2,128)S(1)}, u32[]{:S(2)}, u32[]{:S(2)}) collective-permute-start(s32[4,2,3]{2,1,0:T(2,128)S(1)} %pad_add_fusion), channel_id=1, source_target_pairs={{0,4},{1,5},{2,6},{3,7},{4,0},{5,1},{6,2},{7,3},{8,12},{9,13},{10,... | collective-permute-start | bytes 296 | tf_op jit(solution)/shard_map/ppermute | solution.py:34
  10.2 19.3 %collective-permute-start.4 = (s32[4,2,3]{2,1,0:T(2,128)S(1)}, s32[4,2,3]{2,1,0:T(2,128)S(1)}, u32[]{:S(2)}, u32[]{:S(2)}) collective-permute-start(s32[4,2,3]{2,1,0:T(2,128)S(1)} %pad_add_fusion), channel_id=1, source_target_pairs={{0,8},{1,9},{2,10},{3,11},{4,12},{5,13},{6,14},{7,15},{8,0},{9,1},... | collective-permute-start | bytes 296 | tf_op jit(solution)/shard_map/ppermute | solution.py:34
  11.3 18.3 %collective-permute-start.5 = (s32[4,2,3]{2,1,0:T(2,128)S(1)}, s32[4,2,3]{2,1,0:T(2,128)S(1)}, u32[]{:S(2)}, u32[]{:S(2)}) collective-permute-start(s32[4,2,3]{2,1,0:T(2,128)S(1)} %pad_add_fusion), channel_id=1, source_target_pairs={{0,12},{1,13},{2,14},{3,15},{4,8},{5,9},{6,10},{7,11},{8,4},{9,5},... | collective-permute-start | bytes 296 | tf_op jit(solution)/shard_map/ppermute | solution.py:34
  32.1 3.3 %collective-permute-start.7 = (bf16[16,2,128,128]{3,2,1,0:T(8,128)(2,1)S(1)}, bf16[16,2,128,128]{3,2,1,0:T(8,128)(2,1)S(1)}, u32[]{:S(2)}, u32[]{:S(2)}) collective-permute-start(bf16[16,2,128,128]{3,2,1,0:T(8,128)(2,1)S(1)} %layer_items.3), channel_id=1, source_target_pairs={{0,1},{1,0},{2,3},{3,2},{4,5},{5,4},{6,7},{7,6},{8,9},{9,8},{10,11... | collective-permute-start | bytes 3145736 | tf_op jit(solution)/shard_map/ppermute | solution.py:34
  35.5 6.5 %collective-permute-start.8 = (bf16[2,2,128,128]{3,2,1,0:T(8,128)(2,1)S(1)}, bf16[2,2,128,128]{3,2,1,0:T(8,128)(2,1)S(1)}, u32[]{:S(2)}, u32[]{:S(2)}) collective-permute-start(bf16[2,2,128,128]{3,2,1,0:T(8,128)(2,1)S(1)} %get-tuple-element.38), channel_id=1, source_target_pairs={{0,2},{1,3},{2,0},{3,1},{4,6},{5,7},{6,4},{7,5},{8,10},{9,11},{10,... | collective-permute-start | bytes 393224 | tf_op jit(solution)/shard_map/ppermute | solution.py:34
  35.6 9.0 %copy-start.1 = (f32[16,4,4]{0,2,1:T(4,128)S(1)}, f32[16,4,4]{0,2,1:T(4,128)}, u32[]{:S(2)}) copy-start(f32[16,4,4]{0,2,1:T(4,128)} %param.9) | copy-start | bytes 3076
  35.6 9.3 %collective-permute-start.11 = (bf16[2,2,128,128]{3,2,1,0:T(8,128)(2,1)S(1)}, bf16[2,2,128,128]{3,2,1,0:T(8,128)(2,1)S(1)}, u32[]{:S(2)}, u32[]{:S(2)}) collective-permute-start(bf16[2,2,128,128]{3,2,1,0:T(8,128)(2,1)S(1)} %get-tuple-element.40), channel_id=1, source_target_pairs={{0,4},{1,5},{2,6},{3,7},{4,0},{5,1},{6,2},{7,3},{8,12},{9,13},{10,... | collective-permute-start | bytes 393224 | tf_op jit(solution)/shard_map/ppermute | solution.py:34
  36.5 15.0 %copy-start = (s32[2,3]{1,0:T(2,128)S(1)}, s32[2,3]{1,0:T(2,128)}, u32[]{:S(2)}) copy-start(s32[2,3]{1,0:T(2,128)} %param.11) | copy-start | bytes 76
  36.5 12.7 %collective-permute-start.14 = (bf16[2,2,128,128]{3,2,1,0:T(8,128)(2,1)S(1)}, bf16[2,2,128,128]{3,2,1,0:T(8,128)(2,1)S(1)}, u32[]{:S(2)}, u32[]{:S(2)}) collective-permute-start(bf16[2,2,128,128]{3,2,1,0:T(8,128)(2,1)S(1)} %get-tuple-element.42), channel_id=1, source_target_pairs={{0,2},{1,3},{2,0},{3,1},{4,6},{5,7},{6,4},{7,5},{8,10},{9,11},{10,... | collective-permute-start | bytes 393224 | tf_op jit(solution)/shard_map/ppermute | solution.py:34
  38.7 10.6 %collective-permute-start.16 = (bf16[2,2,128,128]{3,2,1,0:T(8,128)(2,1)S(1)}, bf16[2,2,128,128]{3,2,1,0:T(8,128)(2,1)S(1)}, u32[]{:S(2)}, u32[]{:S(2)}) collective-permute-start(bf16[2,2,128,128]{3,2,1,0:T(8,128)(2,1)S(1)} %get-tuple-element.46), channel_id=1, source_target_pairs={{0,4},{1,5},{2,6},{3,7},{4,0},{5,1},{6,2},{7,3},{8,12},{9,13},{10,... | collective-permute-start | bytes 393224 | tf_op jit(solution)/shard_map/ppermute | solution.py:34
  42.0 8.0 %collective-permute-start.9 = (bf16[1,2,128,128]{3,2,1,0:T(8,128)(2,1)S(1)}, bf16[1,2,128,128]{3,2,1,0:T(8,128)(2,1)S(1)}, u32[]{:S(2)}, u32[]{:S(2)}) collective-permute-start(bf16[1,2,128,128]{3,2,1,0:T(8,128)(2,1)S(1)} %added.11), channel_id=1, source_target_pairs={{0,12},{1,13},{2,14},{3,15},{4,8},{5,9},{6,10},{7,11},{8,4},{9,5},... | collective-permute-start | bytes 196616 | tf_op jit(solution)/shard_map/ppermute | solution.py:34
  44.8 10.3 %collective-permute-start.10 = (bf16[1,2,128,128]{3,2,1,0:T(8,128)(2,1)S(1)}, bf16[1,2,128,128]{3,2,1,0:T(8,128)(2,1)S(1)}, u32[]{:S(2)}, u32[]{:S(2)}) collective-permute-start(bf16[1,2,128,128]{3,2,1,0:T(8,128)(2,1)S(1)} %added.12), channel_id=1, source_target_pairs={{0,8},{1,9},{2,10},{3,11},{4,12},{5,13},{6,14},{7,15},{8,0},{9,1},... | collective-permute-start | bytes 196616 | tf_op jit(solution)/shard_map/ppermute | solution.py:34
  44.9 10.2 %collective-permute-start.12 = (bf16[1,2,128,128]{3,2,1,0:T(8,128)(2,1)S(1)}, bf16[1,2,128,128]{3,2,1,0:T(8,128)(2,1)S(1)}, u32[]{:S(2)}, u32[]{:S(2)}) collective-permute-start(bf16[1,2,128,128]{3,2,1,0:T(8,128)(2,1)S(1)} %added.14), channel_id=1, source_target_pairs={{0,10},{1,11},{2,8},{3,9},{4,14},{5,15},{6,12},{7,13},{8,2},{9,3},... | collective-permute-start | bytes 196616 | tf_op jit(solution)/shard_map/ppermute | solution.py:34
  49.2 6.8 %collective-permute-start.13 = (bf16[1,2,128,128]{3,2,1,0:T(8,128)(2,1)S(1)}, bf16[1,2,128,128]{3,2,1,0:T(8,128)(2,1)S(1)}, u32[]{:S(2)}, u32[]{:S(2)}) collective-permute-start(bf16[1,2,128,128]{3,2,1,0:T(8,128)(2,1)S(1)} %added.15), channel_id=1, source_target_pairs={{0,8},{1,9},{2,10},{3,11},{4,12},{5,13},{6,14},{7,15},{8,0},{9,1},... | collective-permute-start | bytes 196616 | tf_op jit(solution)/shard_map/ppermute | solution.py:34
  49.3 7.3 %collective-permute-start.15 = (bf16[1,2,128,128]{3,2,1,0:T(8,128)(2,1)S(1)}, bf16[1,2,128,128]{3,2,1,0:T(8,128)(2,1)S(1)}, u32[]{:S(2)}, u32[]{:S(2)}) collective-permute-start(bf16[1,2,128,128]{3,2,1,0:T(8,128)(2,1)S(1)} %get-tuple-element.43), channel_id=1, source_target_pairs={{0,4},{1,5},{2,6},{3,7},{4,0},{5,1},{6,2},{7,3},{8,12},{9,13},{10,... | collective-permute-start | bytes 196616 | tf_op jit(solution)/shard_map/ppermute | solution.py:34
  50.0 6.6 %collective-permute-start.17 = (bf16[1,2,128,128]{3,2,1,0:T(8,128)(2,1)S(1)}, bf16[1,2,128,128]{3,2,1,0:T(8,128)(2,1)S(1)}, u32[]{:S(2)}, u32[]{:S(2)}) collective-permute-start(bf16[1,2,128,128]{3,2,1,0:T(8,128)(2,1)S(1)} %get-tuple-element.47), channel_id=1, source_target_pairs={{0,2},{1,3},{2,0},{3,1},{4,6},{5,7},{6,4},{7,5},{8,10},{9,11},{10,... | collective-permute-start | bytes 196616 | tf_op jit(solution)/shard_map/ppermute | solution.py:34
